TPU v7x, 512 devices: a whole 4x8x8 slice. The times are simulated.
512 devices in a mesh: shard: 128 (over z, y, core), rep: 4 (over x).
Axes of the slice: x: 4, y: 8, z: 8, core: 2. Of those that a mesh axis runs over, the one named last changes fastest.
Arguments:
- queries: bfloat16 [4, 128, 32, 128], P('rep', 'shard'), may hold values from -0.5 to 0.5
- candidates: int32 [4, 128, 64], P('rep', 'shard'), may hold values from 0 to 2047, all different within a row; in each aligned block of 128 rows (0 to 127, 128 to 255, ..., all dimensions but the last counted through in order) at most 8 rows name the same one
- codebook: bfloat16 [524288, 128], P(('shard', 'rep')), may hold values from -0.5 to 0.5
- bucket_weights: float32 [4], replicated, may hold values from -0.1 to 0.1
- centroid_ids: int32 [2048, 128], P('shard'), may hold values from 0 to 4095
- residual_codes: int32 [2048, 128, 128], P('shard'), may hold values from 0 to 3
- passage_lengths: int32 [2048], P('shard'), may hold values from 1 to 128, 196608 in all
Outputs:
- best_centroid: float32 [4, 128, 32], P('rep', 'shard')
- scores: float32 [4, 128, 64], P('rep', 'shard')
Inputs may be any that keep to these rules, and one draw needn't show every extreme that they name: `candidates`: each query names 64 different passages. Within the 128 queries of one index of rep, no passage is named by more than 8 queries, a bound that some block reaches. `passage_lengths`: some passage has all 128 slots live.
All inputs are finite; a program needn't handle non-finite values. No bound on the sum of `passage_lengths` on one device may be relied on, other than what follows from the above.
Results may differ from a plain program's by a relative error of at most 0.00045.
Values may be sent and summed in bfloat16 or wider, within the bound.
A program may use at most 64 MiB of HBM per device.

v0:
```python
import math
import jax
import jax.numpy as jnp
from jax import lax
from jax.sharding import PartitionSpec as P

FAR_BELOW = -1e30


def on_device(
    queries, candidates, codebook, bucket_weights, centroid_ids, residual_codes, passage_lengths
):
    feature_width = queries.shape[3]
    query_len = queries.shape[2]
    per_device = queries.shape[1]
    owner_index = lax.axis_index("shard")
    group_queries, group_cands = (
        lax.all_gather(queries, "shard", axis=1, tiled=True),
        lax.all_gather(candidates, "shard", axis=1, tiled=True),
    )
    group_queries = group_queries[0]
    group_cands = group_cands[0]
    group_size = group_queries.shape[0]
    shard_book = lax.all_gather(codebook, "rep", axis=0, tiled=True)
    token_rows = group_queries.reshape(group_size * query_len, feature_width)
    block_rows = math.gcd(token_rows.shape[0], 512)

    def best_block(row_block):
        scored = jnp.dot(row_block, shard_book.T, preferred_element_type=jnp.float32)
        return jnp.max(scored, axis=1)

    partial_best = lax.map(best_block, token_rows.reshape(-1, block_rows, feature_width)).reshape(
        group_size, query_len
    )
    pass_count, pass_len = centroid_ids.shape
    centre_rows = jnp.take(shard_book, centroid_ids.reshape(-1), axis=0).reshape(
        pass_count, pass_len, feature_width
    )
    residual = jnp.zeros(residual_codes.shape, jnp.float32)
    for bucket in range(bucket_weights.shape[0]):
        residual = residual + jnp.where(residual_codes == bucket, bucket_weights[bucket], 0.0)
    decoded = (centre_rows.astype(jnp.float32) + residual).astype(jnp.bfloat16)
    live_mask = jnp.arange(pass_len, dtype=jnp.int32)[None, :] < passage_lengths[:, None]
    flat_tokens = decoded.reshape(pass_count * pass_len, feature_width)
    block_queries = math.gcd(group_size, max(1, 512 // query_len))

    def dense_block(query_block):
        similar = jnp.dot(
            query_block.reshape(-1, feature_width),
            flat_tokens.T,
            preferred_element_type=jnp.float32,
        )
        similar = similar.reshape(block_queries, query_len, pass_count, pass_len)
        similar = jnp.where(live_mask[None, None], similar, FAR_BELOW)
        return jnp.sum(jnp.max(similar, axis=3), axis=1)

    score_table = lax.map(
        dense_block, group_queries.reshape(-1, block_queries, query_len, feature_width)
    ).reshape(group_size, pass_count)
    merged = lax.pmax(partial_best, "shard")
    own_best = lax.dynamic_slice_in_dim(merged, owner_index * per_device, per_device, 0)
    local_index = group_cands - owner_index * pass_count
    picked = jnp.sum(
        jnp.where(
            local_index[:, :, None] == jnp.arange(pass_count, dtype=jnp.int32)[None, None, :],
            score_table[:, None, :],
            0.0,
        ),
        axis=2,
    )
    own_scores = lax.psum_scatter(picked, "shard", scatter_dimension=0, tiled=True)
    return (own_best[None], own_scores[None])


def solution(mesh):
    in_specs = (
        P("rep", "shard", None, None),
        P("rep", "shard", None),
        P(("shard", "rep"), None),
        P(),
        P("shard", None),
        P("shard", None, None),
        P("shard"),
    )
    out_specs = (P("rep", "shard", None), P("rep", "shard", None))
    return jax.shard_map(
        on_device, mesh=mesh, in_specs=in_specs, out_specs=out_specs, check_vma=False
    )
```

profile of v0, /device:TPU:2, one launch (start us, length us, event | category | flops | bytes accessed | tf_op | source)
XLA Modules:
  0.0 1158.6 jit_solution(518266250836284800)
XLA Ops:
  7.2 0.7 all-gather.5.cloned.1.call-update
  7.9 0.7 all-gather.3.cloned.1.call-update
  8.7 50.6 %all_gather.11 = s32[1,128,64]{2,0,1:T(1,128)S(1)} all-gather(s32[1,1,64]{2,0,1:T(1,128)} %bitcast.62), channel_id=1, replica_groups=mesh['shard'=128,'rep'=4] {'shard'}, dimensions={1}, use_global_device_ids=true | all-gather | bytes 33024 | tf_op jit(solution)/shard_map/all_gather | solution.py:19
  59.3 1.3 dynamic-slice
  60.6 1.4 fusion.8
  62.1 0.7 compare_and_fusion
  62.8 0.7 compare_select_fusion
  63.5 7.0 gather_fusion
  70.6 3.1 add_convert_fusion
  73.7 53.1 %all-gather.3.cloned.1.call-done = bf16[1,128,32,128]{3,2,0,1:T(8,128)(2,1)} async-done(((bf16[1,1,32,128]{3,2,0,1:T(8,128)(2,1)}), bf16[1,128,32,128]{3,2,0,1:T(8,128)(2,1)}) %all-gather.3.cloned.1.call-update) | async-done | bytes 1048592 | tf_op jit(solution)/shard_map/all_gather | solution.py:18
  126.8 18.6 %while.21 = (s32[]{:T(128)}, f32[8,512]{1,0:T(8,128)S(1)}, bf16[8,512,128]{2,1,0:T(8,128)(2,1)}, bf16[4096,128]{1,0:T(8,128)(2,1)S(1)}, s32[]{:T(128)}, /*index=5*/s32[]{:T(128)}) while((s32[]{:T(128)}, f32[8,512]{1,0:T(8,128)S(1)}, bf16[8,512,128]{2,1,0:T(8,128)(2,1)}, bf16[4096,128]{1,0:T(8,128)(2,1)S(1)}, s32[]{:T(128)}, ...), condition=%wide.region_2.3_spmd, body=%wide.region_0.2_spmd.sunk | while | flops 538967552 | bytes 1185877 | solution.py:32
  126.8 2.2 convolution_reduce_fusion.2
  129.1 2.2 convolution_reduce_fusion.2
  131.4 2.2 convolution_reduce_fusion.2
  133.7 2.2 convolution_reduce_fusion.2
  136.1 2.2 convolution_reduce_fusion.2
  138.4 2.2 convolution_reduce_fusion.2
  140.7 2.2 convolution_reduce_fusion.2
  143.0 2.2 convolution_reduce_fusion.2
  145.4 493.9 %pmax.7 = f32[128,32]{1,0:T(8,128)S(1)} all-reduce(f32[128,32]{1,0:T(8,128)S(1)} %reshape.69), channel_id=1, replica_groups=mesh['shard'=128,'rep'=4] {'shard'}, use_global_device_ids=true, to_apply=%region_3.4 | all-reduce | flops 4096 | bytes 32768 | tf_op jit(solution)/shard_map/pmax | solution.py:60
  639.3 19.7 %while.22 = (s32[]{:T(128)}, f32[8,16,16]{2,1,0:T(8,128)S(1)}, bf16[8,16,32,128]{3,2,1,0:T(8,128)(2,1)}, bf16[2048,128]{1,0:T(8,128)(2,1)S(1)}, s32[16]{0:T(128)S(1)}, /*index=5*/s32[]{:T(128)}, f32[]{:T(128)}) while((s32[]{:T(128)}, f32[8,16,16]{2,1,0:T(8,128)S(1)}, bf16[8,16,32,128]{3,2,1,0:T(8,128)(2,1)}, ...), condition=%wide.region_7.8_spmd.clone, body=%wide.region_4.7_spmd.clone.sunk | while | flops 270534400 | bytes 742561 | solution.py:57
  639.4 2.2 select_reduce_fusion.3
  641.8 2.2 select_reduce_fusion.3
  644.3 2.2 select_reduce_fusion.3
  646.8 2.2 select_reduce_fusion.3
  649.2 2.2 select_reduce_fusion.3
  651.7 2.2 select_reduce_fusion.3
  654.1 2.2 select_reduce_fusion.3
  656.6 2.2 select_reduce_fusion.3
  659.3 490.9 %all-reduce = f32[128,64]{1,0:T(8,128)S(1)} all-reduce(f32[128,64]{1,0:T(8,128)S(1)} %copy.15), channel_id=2, replica_groups=mesh['shard'=128,'rep'=4] {'shard'}, use_global_device_ids=true, to_apply=%region_9.10.clone | all-reduce | flops 8192 | bytes 65536
  1150.1 0.5 dynamic-slice_bitcast_fusion.1
  1150.7 1.1 dynamic-slice_bitcast_fusion
  (50 shorter events, 2.5 us)
Async XLA Ops:
  7.2 56.4 %all-gather.5.cloned.1.call-start = ((), (), s32[]{:S(2)}) async-start(), calls=%async_computation.1 | async-start | bytes 1310720 | tf_op jit(solution)/shard_map/all_gather | solution.py:24
  7.9 118.9 %all-gather.3.cloned.1.call-start = ((), (), s32[]{:S(2)}) async-start(), calls=%async_computation | async-start | bytes 1056768 | tf_op jit(solution)/shard_map/all_gather | solution.py:18
  63.5 7.1 copy-start.1
  70.6 56.2 %copy-start = (bf16[4096,128]{1,0:T(8,128)(2,1)S(1)}, bf16[4096,128]{1,0:T(8,128)(2,1)}, u32[]{:S(2)}) copy-start(bf16[4096,128]{1,0:T(8,128)(2,1)} %all-gather.5.cloned.1.call-done) | copy-start | bytes 3145732
  126.8 512.6 %copy-start.2 = (s32[16]{0:T(128)S(1)}, s32[16]{0:T(128)}, u32[]{:S(2)}) copy-start(s32[16]{0:T(128)} %param.17) | copy-start | bytes 196
Sparse Core Ops, SparseCore 0:
  10.1 33.0 all-gather.4
  46.2 80.5 all-gather.2
where the time goes:
time: 1160 us
  blocking collectives  1040 us (90%)
  waiting for transfers between devices  54.5 us (5%)
  matrix products  35.8 us (3%)
  between operations  14.2 us (1%)
  local copies, waits for them, and re-layouts  12.2 us (1%)
    pmax x1, blocking collectives, on_device(): merged = lax.pmax(partial_best, 'shard')  494 us
    unnamed x1, blocking collectives  491 us
    all_gather x1, waiting for transfers between devices, on_device(): lax.all_gather(queries, 'shard', axis=1, tiled=True)  53.1 us
    all_gather x1, blocking collectives, on_device(): lax.all_gather(candidates, 'shard', axis=1, tiled=True)  50.6 us
  transfers between devices with their start and end apart: 2, of which 1 were waited for; matrix products, arithmetic and copies ran while one was open for 1% of the time, Pallas kernels for 0%

commit v1 on v0

--- a/solution.py
+++ b/solution.py
@@ -16,7 +16,9 @@
     owner_index = lax.axis_index("shard")
     group_queries, group_cands = (
         lax.all_gather(queries, "shard", axis=1, tiled=True),
-        lax.all_gather(candidates, "shard", axis=1, tiled=True),
+        jnp.concatenate(
+            lax.all_to_all(jnp.stack([candidates] * lax.axis_size("shard")), "shard", 0, 0), axis=1
+        ),
     )
     group_queries = group_queries[0]
     group_cands = group_cands[0]

time: 1160 us -> 1160 us (level)
  blocking collectives: 1040 us -> 985 us
  waiting for transfers between devices: 54.5 us -> 85.7 us
  starting transfers between devices: 0.08 us -> 17.9 us
    all_gather x1 -> x0, blocking collectives: 50.6 us -> none  [on_device(): lax.all_gather(candidates, 'shard', axis=1, tiled=True)]
    all_gather x1, waiting for transfers between devices: 53.1 us -> 73.7 us  [on_device(): lax.all_gather(queries, 'shard', axis=1, tiled=True)]
    all_to_all x0 -> x1, starting transfers between devices: none -> 17.8 us  [on_device(): lax.all_to_all(jnp.stack([candidates] * lax.axis_size('shard')), 'shard',...]
  transfers between devices with their start and end apart: 2 -> 3, of which waited for: 1 -> 3; matrix products, arithmetic and copies ran while one was open for 1% -> 1% of each run, Pallas kernels for 0% -> 0%
where the time goes in v1:
time: 1160 us
  blocking collectives  985 us (85%)
  waiting for transfers between devices  85.7 us (7%)
  matrix products  35.8 us (3%)
  starting transfers between devices  17.9 us (2%)
  between operations  14.2 us (1%)
  local copies, waits for them, and re-layouts  13.5 us (1%)
    pmax x1, blocking collectives, on_device(): merged = lax.pmax(partial_best, 'shard')  494 us
    unnamed x1, blocking collectives  491 us
    all_gather x1, waiting for transfers between devices, on_device(): lax.all_gather(queries, 'shard', axis=1, tiled=True)  73.7 us
  transfers between devices with their start and end apart: 3, of which 3 were waited for; matrix products, arithmetic and copies ran while one was open for 1% of the time, Pallas kernels for 0%

profile of v1, /device:TPU:2, one launch (start us, length us, event | category | flops | bytes accessed | tf_op | source)
XLA Modules:
  0.0 1158.6 jit_solution(16684823741266100749)
XLA Ops:
  8.6 1.3 stack.2
  10.0 17.8 %all-to-all-start = ((s32[128,1,1,64]{3,2,1,0:T(1,128)}), s32[128,1,1,64]{3,2,1,0:T(1,128)S(1)}, u32[]{:S(2)}, u32[]{:S(2)}) async-start(s32[128,1,1,64]{3,2,1,0:T(1,128)} %stack.2), calls=%async_computation | async-start | bytes 131072 | tf_op jit(solution)/shard_map/all_to_all | solution.py:20
  27.8 1.3 dynamic-slice
  29.1 0.7 compare_and_fusion
  29.8 0.7 compare_select_fusion
  30.6 1.5 fusion.8
  32.0 6.9 all-to-all-done
  39.0 3.8 all-gather.5.cloned.1.call-done
  42.8 7.0 gather_fusion
  49.8 3.2 add_convert_fusion
  53.0 73.7 %all-gather.3.cloned.1.call-done = bf16[1,128,32,128]{3,2,0,1:T(8,128)(2,1)} async-done(((bf16[1,1,32,128]{3,2,0,1:T(8,128)(2,1)}), bf16[1,128,32,128]{3,2,0,1:T(8,128)(2,1)}) %all-gather.3.cloned.1.call-update) | async-done | bytes 1048592 | tf_op jit(solution)/shard_map/all_gather | solution.py:18
  126.8 18.6 %while.21 = (s32[]{:T(128)}, f32[8,512]{1,0:T(8,128)S(1)}, bf16[8,512,128]{2,1,0:T(8,128)(2,1)}, bf16[4096,128]{1,0:T(8,128)(2,1)S(1)}, s32[]{:T(128)}, /*index=5*/s32[]{:T(128)}) while((s32[]{:T(128)}, f32[8,512]{1,0:T(8,128)S(1)}, bf16[8,512,128]{2,1,0:T(8,128)(2,1)}, bf16[4096,128]{1,0:T(8,128)(2,1)S(1)}, s32[]{:T(128)}, ...), condition=%wide.region_2.3_spmd, body=%wide.region_0.2_spmd.sunk | while | flops 538967552 | bytes 1185877 | solution.py:34
  126.8 2.2 convolution_reduce_fusion.2
  129.1 2.2 convolution_reduce_fusion.2
  131.4 2.2 convolution_reduce_fusion.2
  133.7 2.2 convolution_reduce_fusion.2
  136.1 2.2 convolution_reduce_fusion.2
  138.4 2.2 convolution_reduce_fusion.2
  140.7 2.2 convolution_reduce_fusion.2
  143.0 2.2 convolution_reduce_fusion.2
  145.4 493.9 %pmax.7 = f32[128,32]{1,0:T(8,128)S(1)} all-reduce(f32[128,32]{1,0:T(8,128)S(1)} %reshape.72), channel_id=1, replica_groups=mesh['shard'=128,'rep'=4] {'shard'}, use_global_device_ids=true, to_apply=%region_3.4 | all-reduce | flops 4096 | bytes 32768 | tf_op jit(solution)/shard_map/pmax | solution.py:62
  639.3 19.7 %while.22 = (s32[]{:T(128)}, f32[8,16,16]{2,1,0:T(8,128)S(1)}, bf16[8,16,32,128]{3,2,1,0:T(8,128)(2,1)}, bf16[2048,128]{1,0:T(8,128)(2,1)S(1)}, s32[16]{0:T(128)S(1)}, /*index=5*/s32[]{:T(128)}, f32[]{:T(128)}) while((s32[]{:T(128)}, f32[8,16,16]{2,1,0:T(8,128)S(1)}, bf16[8,16,32,128]{3,2,1,0:T(8,128)(2,1)}, ...), condition=%wide.region_7.8_spmd.clone, body=%wide.region_4.7_spmd.clone.sunk | while | flops 270534400 | bytes 742561 | solution.py:59
  639.4 2.2 select_reduce_fusion.3
  641.8 2.2 select_reduce_fusion.3
  644.3 2.2 select_reduce_fusion.3
  646.8 2.2 select_reduce_fusion.3
  649.2 2.2 select_reduce_fusion.3
  651.7 2.2 select_reduce_fusion.3
  654.1 2.2 select_reduce_fusion.3
  656.6 2.2 select_reduce_fusion.3
  659.3 490.9 %all-reduce = f32[128,64]{1,0:T(8,128)S(1)} all-reduce(f32[128,64]{1,0:T(8,128)S(1)} %copy.16), channel_id=2, replica_groups=mesh['shard'=128,'rep'=4] {'shard'}, use_global_device_ids=true, to_apply=%region_9.10.clone | all-reduce | flops 8192 | bytes 65536
  1150.7 1.1 dynamic-slice_bitcast_fusion
  (52 shorter events, 4.4 us)
Async XLA Ops:
  7.2 35.6 %all-gather.5.cloned.1.call-start = ((), (), s32[]{:S(2)}) async-start(), calls=%async_computation.2 | async-start | bytes 1310720 | tf_op jit(solution)/shard_map/all_gather | solution.py:26
  7.9 118.9 %all-gather.3.cloned.1.call-start = ((), (), s32[]{:S(2)}) async-start(), calls=%async_computation.1 | async-start | bytes 1056768 | tf_op jit(solution)/shard_map/all_gather | solution.py:18
  10.0 28.9 %all-to-all-start = ((s32[128,1,1,64]{3,2,1,0:T(1,128)}), s32[128,1,1,64]{3,2,1,0:T(1,128)S(1)}, u32[]{:S(2)}, u32[]{:S(2)}) async-start(s32[128,1,1,64]{3,2,1,0:T(1,128)} %stack.2), calls=%async_computation | async-start | bytes 131072 | tf_op jit(solution)/shard_map/all_to_all | solution.py:20
  39.0 10.8 copy-start.1
  49.8 77.0 %copy-start = (bf16[4096,128]{1,0:T(8,128)(2,1)S(1)}, bf16[4096,128]{1,0:T(8,128)(2,1)}, u32[]{:S(2)}) copy-start(bf16[4096,128]{1,0:T(8,128)(2,1)} %all-gather.5.cloned.1.call-done) | copy-start | bytes 3145732
  126.8 512.6 %copy-start.2 = (s32[16]{0:T(128)S(1)}, s32[16]{0:T(128)}, u32[]{:S(2)}) copy-start(s32[16]{0:T(128)} %param.17) | copy-start | bytes 196
Sparse Core Ops, SparseCore 0:
  10.1 32.6 all-gather.4
  45.8 80.8 all-gather.2
